TPU v7x, 256 devices: a whole 4x4x8 slice. The times are simulated.
256 devices in a mesh: section: 32 (over z, y_lo, core), dp: 8 (over x, y_hi).
Axes of the slice: x: 4, y: 4 (y_hi: 2, y_lo: 2; y = y_hi * 2 + y_lo), z: 8, core: 2. Of those that a mesh axis runs over, the one named last changes fastest.
Arguments:
- entry_codes: bfloat16 [4, 128, 12288], P(None, 'dp', 'section'), may hold values from -16 to 16
- loss_target: bfloat16 [4, 128, 12288], P(None, 'dp', 'section'), may hold values from -6 to 6
- fwd_inflow: bfloat16 [32, 128, 12288], P('section', 'dp'), may hold values from -16 to 16
- bwd_inflow: bfloat16 [32, 128, 12288], P('section', 'dp'), may hold values from -16 to 16
- act_cache: bfloat16 [32, 32, 16, 12288], P('section', 'dp'), may hold values from -6 to 6
- act_exps: int32 [32, 32, 16, 96], P('section', 'dp'), may hold values from -5 to -1
- grad_cache: bfloat16 [32, 32, 16, 12288], P('section', 'dp'), may hold values from -6 to 6
- grad_exps: int32 [32, 32, 16, 96], P('section', 'dp'), may hold values from -5 to -1
- fwd_rows: int32 [32, 32], P('section', 'dp'), may hold values from 0 to 3, as said below
- bwd_rows: int32 [32, 32], P('section', 'dp'), may hold values from 0 to 3, as said below
- norm_gain: bfloat16 [32, 12288], P('section'), may hold values from 0.5 to 2
- w_in: bfloat16 [32, 64, 12288], P('section'), may hold values from -0.0546875 to 0.0546875
- w_out: bfloat16 [32, 64, 12288], P('section'), may hold values from -0.75 to 0.75
Outputs:
- grad_w_in: bfloat16 [32, 64, 12288], P('section', None, 'dp')
- grad_w_out: bfloat16 [32, 64, 12288], P('section', None, 'dp')
- grad_gain: float32 [32, 12288], P('section', 'dp')
- fwd_outflow: bfloat16 [32, 128, 12288], P('section', 'dp')
- bwd_outflow: bfloat16 [32, 128, 12288], P('section', 'dp')
Inputs may be any that keep to these rules, and one draw needn't show every extreme that they name: `fwd_rows`: each aligned block of 4 entries (one section, one data replica) names every row 0 to 3 once. `bwd_rows`: each aligned block of 4 entries (one section, one data replica) names every row 0 to 3 once.
All inputs are finite; a program needn't handle non-finite values.
Results may differ from a plain program's by a relative error of at most 0.017.
Values may be sent and summed in bfloat16 or wider, within the bound.
A program may use at most 128 MiB of HBM per device.

v0:
```python
import functools

import jax
import jax.numpy as jnp
from jax import lax
from jax.experimental import pallas as pl
from jax.experimental.pallas import tpu as pltpu
from jax.sharding import PartitionSpec as P

MESH = pl.DeviceIdType.MESH
ROWS = 16
TICKS = 4
VMEM_BYTES = 64 * 1024 * 1024
OPEN = 3e38
F32 = jnp.float32
BF16 = jnp.bfloat16


def dot_last(a, b):
    return lax.dot_general(a, b, (((1,), (1,)), ((), ())), preferred_element_type=F32)


def dot_first(a, b):
    return lax.dot_general(a, b, (((0,), (0,)), ((), ())), preferred_element_type=F32)


def dot_plain(a, b):
    return lax.dot_general(a, b, (((1,), (0,)), ((), ())), preferred_element_type=F32)


def lane_sums(x):
    x = x.astype(F32)
    x = x * x
    return sum(x[:, i : i + 128] for i in range(0, x.shape[1], 128))


def half_erf(u):
    return 0.5 * (1.0 + lax.erf(u * 0.7071067811865476))


def gelu(u):
    return u * half_erf(u)


def gelu_slope(u):
    return half_erf(u) + u * jnp.exp(-0.5 * u * u) * 0.3989422804014327


def kernel(
    sections,
    replicas,
    fwd_rows_hbm,
    bwd_rows_hbm,
    gain_hbm,
    act_exps_hbm,
    grad_exps_hbm,
    entry_hbm,
    target_hbm,
    fwd_inflow,
    bwd_inflow,
    act_hbm,
    grad_hbm,
    w_in_hbm,
    w_out_hbm,
    gw_in_out,
    gw_out_out,
    ggain_out,
    fwd_out,
    bwd_out,
    fwd_rows,
    bwd_rows,
    gain_ref,
    act_exps,
    grad_exps,
    inputs,
    grad,
    w_in,
    w_out,
    wg,
    fwd_code,
    bwd_code,
    entries,
    targets,
    lim_act,
    lim_grad,
    x_now,
    g_all,
    y_send,
    y_recv,
    d_send,
    d_recv,
    u_back,
    slope_back,
    r_back,
    a_back,
    du_tick,
    factors,
    x_gather,
    g_gather,
    f_gather,
    p_send,
    p_recv,
    load_sem,
    mail,
    mail_sem,
    entry_send,
    entry_recv,
    y_send_sem,
    y_recv_sem,
    d_send_sem,
    d_recv_sem,
    x_send_sem,
    x_recv_sem,
    g_send_sem,
    g_recv_sem,
    f_send_sem,
    f_recv_sem,
    p_send_sem,
    p_recv_sem,
    out_sem,
):
    width = w_in.shape[1]
    ring = replicas // 2
    cut = width // ring
    share = width // replicas
    piece = width // sections
    inv_width = 1.0 / width
    act = inputs.at[0]
    s = lax.axis_index("section")
    p = lax.axis_index("dp")
    px = p // 2
    py = p % 2
    first = s == 0
    last = s == sections - 1
    x_from = jnp.where(last, 1, 0)
    not_first = s > 0
    not_last = s < sections - 1
    mate = px * 2 + (1 - py)
    side = s // 2 % 2
    partner = s + 2 - 4 * side

    barrier = pltpu.get_barrier_semaphore()

    def greet(where):
        pl.semaphore_signal(barrier, inc=1, device_id=where, device_id_type=MESH)

    @pl.when(not_first)
    def _():
        greet({"section": s - 1})

    @pl.when(not_last)
    def _():
        greet({"section": s + 1})

    for k in range(1, ring):
        greet({"dp": lax.rem(px + k, ring) * 2 + py})
    greet({"dp": mate})
    greet({"section": partner})

    @pl.when(first)
    def _():
        def tell(i, c):
            greet({"section": i})
            return c

        lax.fori_loop(1, sections, tell, 0)

    @pl.when(last)
    def _():
        def tell(i, c):
            greet({"section": i})
            return c

        lax.fori_loop(0, sections - 1, tell, 0)

    loads = [
        pltpu.make_async_copy(src, dst, load_sem.at[i])
        for i, (src, dst) in enumerate(
            [
                (act_hbm, act),
                (w_in_hbm, w_in),
                (fwd_inflow, fwd_code),
                (w_out_hbm, w_out),
                (grad_hbm, grad),
                (bwd_inflow, bwd_code),
                (fwd_rows_hbm, fwd_rows),
                (bwd_rows_hbm, bwd_rows),
                (gain_hbm, gain_ref),
                (act_exps_hbm, act_exps),
                (grad_exps_hbm, grad_exps),
            ]
        )
    ]
    for i in (9, 10, 8, 6, 7, 1, 0):
        loads[i].start()

    @pl.when(s % 2 == 1)
    def _():
        for i in (2, 3, 4, 5):
            loads[i].start()

    @pl.when(s % 2 == 0)
    def _():
        for i in (4, 5, 3, 2):
            loads[i].start()

    count = (
        jnp.where(not_first, 2, 0) + jnp.where(not_last, 2, 0) + (ring - 1) + 2
    )
    pl.semaphore_wait(barrier, count)

    def mine(owner):
        return pl.ds(pl.multiple_of(owner * piece, 128), piece)

    def mail_copy(src):
        at = pl.ds(1, TICKS - 1)
        return pltpu.make_async_remote_copy(
            src_ref=src.at[at],
            dst_ref=mail.at[at],
            send_sem=mail_sem.at[0],
            recv_sem=mail_sem.at[1],
            device_id={"section": partner},
            device_id_type=MESH,
        )

    def entry_copy(which, t, from_mail):
        src = mail if from_mail else (entry_hbm, target_hbm)[which]
        dst = (entries, targets)[which]
        return pltpu.make_async_remote_copy(
            src_ref=src.at[t],
            dst_ref=dst.at[t, :, mine(partner if from_mail else s)],
            send_sem=entry_send.at[from_mail if t > 0 else which, t],
            recv_sem=entry_recv.at[which, t],
            device_id={"section": (0, sections - 1)[which]},
            device_id_type=MESH,
        )

    def entry_local(which, t, from_mail):
        src = mail if from_mail else (entry_hbm, target_hbm)[which]
        dst = (entries, targets)[which]
        return pltpu.make_async_copy(
            src.at[t],
            dst.at[t, :, mine(partner if from_mail else s)],
            entry_recv.at[which, t],
        )

    def entry_wait(which, t):
        dst = (entries, targets)[which]
        pltpu.make_async_copy(dst.at[t], dst.at[t], entry_recv.at[which, t]).wait()

    direct = ((0, not_first, first), (1, not_last, last))
    ends = ((0, (side == 0) & not_first, first), (1, (side == 1) & not_last, last))

    def start_entries(t, from_mail):
        for which, away, here in direct if t == 0 else ends:

            @pl.when(away)
            def _():
                entry_copy(which, t, from_mail).start()

            @pl.when(here)
            def _():
                entry_local(which, t, from_mail).start()

    start_entries(0, 0)

    @pl.when(side == 0)
    def _():
        mail_copy(target_hbm).start()

    @pl.when(side == 1)
    def _():
        mail_copy(entry_hbm).start()

    def columns(j):
        return pl.ds(pl.multiple_of(j * cut, 128), cut)

    def half_columns(j, part):
        half = 1 - py if part == 0 else py
        return pl.ds(pl.multiple_of(j * cut + half * share, 128), share)

    def spread(refs, slot, j, part, src=None):
        held, dst, send_sem, recv_sem = refs
        src = held if src is None else src
        index = slot * 2 + part

        @pl.when(j != px)
        def _():
            pltpu.make_async_remote_copy(
                src_ref=src.at[slot, :, half_columns(j, part)],
                dst_ref=dst.at[px, slot, :, half_columns(0, part)],
                send_sem=send_sem.at[index, j],
                recv_sem=recv_sem.at[px, index],
                device_id={"dp": j * 2 + py},
                device_id_type=MESH,
            ).start()

        @pl.when(j == px)
        def _():
            pltpu.make_async_copy(
                src.at[slot, :, half_columns(j, part)],
                dst.at[px, slot, :, half_columns(0, part)],
                recv_sem.at[px, index],
            ).start()

    def spread_all(refs, slot, part, src=None):
        for k in range(ring):
            spread(refs, slot, lax.rem(px + k, ring), part, src)

    def spread_wait(refs, part):
        src, dst, send_sem, recv_sem = refs

        def one(i, c):
            slot, k = i // ring, i % ring
            index = slot * 2 + part

            @pl.when(k != px)
            def _():
                copy = pltpu.make_async_remote_copy(
                    src_ref=src.at[slot, :, half_columns(k, part)],
                    dst_ref=dst.at[k, slot, :, half_columns(0, part)],
                    send_sem=send_sem.at[index, k],
                    recv_sem=recv_sem.at[k, index],
                    device_id={"dp": k * 2 + py},
                    device_id_type=MESH,
                )
                copy.wait_recv()
                copy.wait_send()

            @pl.when(k == px)
            def _():
                pltpu.make_async_copy(
                    src.at[slot, :, half_columns(k, part)],
                    dst.at[k, slot, :, half_columns(0, part)],
                    recv_sem.at[k, index],
                ).wait()

            return c

        lax.fori_loop(0, ring * TICKS, one, 0)

    x_refs = (inputs.at[1], x_gather, x_send_sem, x_recv_sem)
    g_refs = (g_all, g_gather, g_send_sem, g_recv_sem)

    @pl.when(not_last)
    def _():
        for slot in range(TICKS):
            spread_all(x_refs, slot, 0, act_hbm)

    blocks = act_exps.shape[-1]

    def expand(exps, rows, limits, t):
        scale = jnp.exp2(exps[rows[0, t]].astype(F32) + 4.0)
        for j in range(ring):
            limits[t, :, j * cut : (j + 1) * cut] = jnp.concatenate(
                [
                    jnp.broadcast_to(scale[:, b : b + 1], (ROWS, 128))
                    for b in range(j * blocks // ring, (j + 1) * blocks // ring)
                ],
                axis=1,
            ).astype(BF16)

    def expand_forward(t):
        expand(act_exps, fwd_rows, lim_act, t)

    def expand_backward(t):
        expand(grad_exps, bwd_rows, lim_grad, t)

    loads[1].wait()
    loads[8].wait()

    def fold(j, c):
        wg[:, columns(j)] = (
            w_in[:, columns(j)].astype(F32) * gain_ref[:, columns(j)].astype(F32)
        ).astype(BF16)
        return c

    lax.fori_loop(0, ring, fold, 0)

    def pass_entries():
        start_entries(1, 0)
        mail_copy(target_hbm).wait()
        start_entries(1, 1)

    @pl.when(last)
    def _():
        pass_entries()
    for i in (0, 6, 7, 9, 10):
        loads[i].wait()

    def y_copy(t, j):
        return pltpu.make_async_remote_copy(
            src_ref=y_send.at[t, :, columns(j)],
            dst_ref=y_recv.at[t, :, columns(j)],
            send_sem=y_send_sem.at[t, j],
            recv_sem=y_recv_sem.at[t, j],
            device_id={"section": s + 1},
            device_id_type=MESH,
        )

    def d_copy(t, j):
        return pltpu.make_async_remote_copy(
            src_ref=d_send.at[t, :, columns(j)],
            dst_ref=d_recv.at[t, :, columns(j)],
            send_sem=d_send_sem.at[t, j],
            recv_sem=d_recv_sem.at[t, j],
            device_id={"section": s - 1},
            device_id_type=MESH,
        )

    def scaled(cache, limit, code):
        return (
            cache.astype(F32) + limit.astype(F32) * 0.0625 * code.astype(F32)
        ).astype(BF16)

    def clipped(cache, limit, value):
        return jnp.minimum(jnp.maximum(value, cache - limit), cache + limit)

    def forward(t):
        row = fwd_rows[0, t]

        @pl.when(first)
        def _():
            entry_wait(0, t)
            if t > 0:
                y_recv[t - 1] = scaled(act[row], lim_act[t], entries[t])
                lim_act[t] = jnp.full((ROWS, width), OPEN, BF16)

        def take(j, c):
            total, u = c
            at = columns(j)
            cache, limit = act[row, :, at], lim_act[t, :, at]
            if t == 0:

                @pl.when(first)
                def _():
                    x_now[:, at] = scaled(cache, limit, entries[t, :, at])

                @pl.when(not_first)
                def _():
                    x_now[:, at] = scaled(cache, limit, fwd_code[:, at])

                x = x_now[:, at]
            else:

                @pl.when(not_first)
                def _():
                    y_copy(t - 1, j).wait_recv()

                x = clipped(cache, limit, y_recv[t - 1, :, at])
                x_now[:, at] = x

            total = total + lane_sums(x)
            u = u + dot_last(x, wg[:, at])

            @pl.when(last)
            def _():
                inputs[1, t, :, at] = x
                spread(x_refs, t, j, 0)
                spread(x_refs, t, j, 1)

            return total, u

        total, u = lax.fori_loop(
            0,
            ring,
            take,
            (jnp.zeros((ROWS, 128), F32), jnp.zeros((ROWS, w_in.shape[0]), F32)),
        )
        total = jnp.sum(total, axis=1, keepdims=True)
        r = lax.rsqrt(total * inv_width + 1e-05)
        u = u * r
        a = gelu(u).astype(BF16)

        @pl.when(last)
        def _():
            u_back[t] = u
            r_back[t] = jnp.broadcast_to(r, (ROWS, 128))
            a_back[t] = a
            slope_back[t] = gelu_slope(u)
            entry_wait(1, t)

        def give(j, c):
            at = columns(j)
            y = x_now[:, at].astype(F32) + dot_plain(a, w_out[:, at])
            y_send[t, :, at] = y.astype(BF16)
            if t < TICKS - 1:

                @pl.when(not_last)
                def _():
                    y_copy(t, j).start()

            @pl.when(last)
            def _():
                g = (y - targets[t, :, at].astype(F32)).astype(BF16)
                if t == 0:
                    g_all[t, :, at] = g
                else:
                    d_recv[t - 1, :, at] = g

            return c

        lax.fori_loop(0, ring, give, 0)
        if t == TICKS - 1:
            pltpu.make_async_copy(y_send.at[t], fwd_out, out_sem.at[0]).start()

    def prepare_backward():
        def take(j, c):
            total, u = c
            at = columns(j)
            x = inputs[0, :, :, at].reshape(TICKS * ROWS, cut)
            return total + lane_sums(x), u + dot_last(x, wg[:, at])

        total, u = lax.fori_loop(
            0,
            ring,
            take,
            (
                jnp.zeros((TICKS * ROWS, 128), F32),
                jnp.zeros((TICKS * ROWS, w_in.shape[0]), F32),
            ),
        )
        total = jnp.sum(total, axis=1, keepdims=True)
        r = lax.rsqrt(total * inv_width + 1e-05)
        u = u * r
        slope_back[...] = gelu_slope(u).reshape(slope_back.shape)
        u_back[...] = u.reshape(u_back.shape)
        r_back[...] = jnp.broadcast_to(r, (TICKS * ROWS, 128)).reshape(r_back.shape)
        a_back[...] = gelu(u).astype(BF16).reshape(a_back.shape)

    def spread_later(t):
        for slot in ((), (0,), (1,), (2, 3))[t]:
            spread_all(g_refs, slot, 1)

        @pl.when(not_last)
        def _():
            for slot in ((0,), (1,), (2,), (3,))[t]:
                spread_all(x_refs, slot, 1, act_hbm)

    def backward_take(t):
        row = bwd_rows[0, t]
        used = jnp.where(last, t, row)

        def take(j, c):
            at = columns(j)

            cache, limit = grad[row, :, at], lim_grad[t, :, at]
            if t == 0:

                @pl.when(not_last)
                def _():
                    g_all[t, :, at] = scaled(cache, limit, bwd_code[:, at])

                g = g_all[t, :, at]
            else:

                @pl.when(not_last)
                def _():
                    d_copy(t - 1, j).wait_recv()

                g = clipped(cache, limit, d_recv[t - 1, :, at])
                g_all[t, :, at] = g
            if t < TICKS - 1:
                spread(g_refs, t, j, 0)
            return c + dot_last(g, w_out[:, at])

        d_active = lax.fori_loop(
            0, ring, take, jnp.zeros((ROWS, w_in.shape[0]), F32)
        )
        if t < TICKS - 1:
            spread_later(t)
        u = u_back[used]
        r = r_back[used][:, :1]
        du = d_active * slope_back[used]
        shift = r * r * (jnp.sum(du * u, axis=1, keepdims=True) * inv_width)
        du_tick[t] = (du * r).astype(BF16)
        factors[1, t] = a_back[used]
        return used, r, shift, du.astype(BF16)

    def backward_give(t, held):
        used, r, shift, du = held

        def give(j, c):
            at = columns(j)
            dx = (
                g_all[t, :, at].astype(F32)
                + r * dot_plain(du, wg[:, at])
                - inputs[x_from, used, :, at].astype(F32) * shift
            )
            d_send[t, :, at] = dx.astype(BF16)
            if t < TICKS - 1:

                @pl.when(not_first)
                def _():
                    d_copy(t, j).start()

            return c

        lax.fori_loop(0, ring, give, 0)
        if t == TICKS - 1:
            pltpu.make_async_copy(d_send.at[t], bwd_out, out_sem.at[1]).start()

    def factor_copy(to, frm):
        return pltpu.make_async_remote_copy(
            src_ref=factors,
            dst_ref=f_gather.at[frm],
            send_sem=f_send_sem.at[to],
            recv_sem=f_recv_sem.at[frm],
            device_id={"dp": to * 2 + py},
            device_id_type=MESH,
        )

    def backward(t):
        backward_give(t, backward_take(t))

    def send_factors():
        used = [jnp.where(last, t, bwd_rows[0, t]) for t in range(TICKS)]
        for q in range(TICKS):
            at = 0
            for t in range(1, TICKS):
                at = jnp.where(used[t] == q, t, at)
            factors[0, q] = du_tick[at]
        for k in range(1, ring):
            factor_copy(lax.rem(px + k, ring), px).start()
        pltpu.make_async_copy(factors, f_gather.at[px], f_recv_sem.at[px]).start()

    rows = ring * TICKS * ROWS
    win = w_in.shape[0]

    def product(which, half):
        at = pl.ds(pl.multiple_of(half * share, 128), share)
        data = (x_gather, g_gather)[which]
        return dot_first(
            f_gather[:, which].reshape(rows, win),
            data[:, :, :, at].reshape(rows, share),
        )

    def swap(which):
        return pltpu.make_async_remote_copy(
            src_ref=p_send.at[which],
            dst_ref=p_recv.at[which],
            send_sem=p_send_sem.at[which],
            recv_sem=p_recv_sem.at[which],
            device_id={"dp": mate},
            device_id_type=MESH,
        )

    def give_product(which):
        p_send[which] = product(which, 1 - py).astype(BF16)
        swap(which).start()

    def spread_last_gradient():
        spread_all(g_refs, TICKS - 1, 0)
        spread_later(TICKS - 1)

    def first_products():
        pltpu.make_async_copy(factors, f_gather.at[px], f_recv_sem.at[px]).wait()
        for k in range(1, ring):
            other = lax.rem(px + k, ring)
            factor_copy(other, other).wait()
        spread_wait(x_refs, 0)
        give_product(0)

    def second_products():
        spread_wait(g_refs, 0)
        give_product(1)

    def rest_of_limits():
        def one(t, c):
            expand_forward(t)
            expand_backward(t)
            return c

        lax.fori_loop(1, TICKS, one, 0)

        @pl.when(last)
        def _():
            for t in range(1, TICKS):
                lim_grad[t] = jnp.full((ROWS, width), OPEN, BF16)

    def more_entries(t):
        start_entries(t, 0)
        start_entries(t, 1)

    @pl.when(last)
    def _():
        for i in (2, 3, 4, 5):
            loads[i].wait()
        expand_forward(0)
        forward(0)
        backward(0)
        more_entries(2)
        more_entries(3)
        rest_of_limits()
        for t in range(1, TICKS - 1):
            forward(t)
            backward(t)
        forward(TICKS - 1)
        held = backward_take(TICKS - 1)
        send_factors()
        spread_last_gradient()
        backward_give(TICKS - 1, held)
        first_products()
        second_products()

    @pl.when(not_last)
    def _():
        @pl.when(s % 2 == 1)
        def _():
            for i in (2, 3):
                loads[i].wait()
            expand_forward(0)
            forward(0)
            pass_entries()
            for i in (4, 5):
                loads[i].wait()
            prepare_backward()
            expand_backward(0)
            backward(0)

        @pl.when(s % 2 == 0)
        def _():
            for i in (4, 5, 3):
                loads[i].wait()
            prepare_backward()
            expand_backward(0)
            backward(0)
            pass_entries()
            loads[2].wait()
            expand_forward(0)
            forward(0)

        more_entries(2)
        more_entries(3)
        rest_of_limits()

        @pl.when(s % 2 == 1)
        def _():
            forward(1)
            backward(1)

        @pl.when(s % 2 == 0)
        def _():
            backward(1)
            forward(1)

        backward(2)
        forward(2)

        @pl.when(s % 2 == 1)
        def _():
            forward(TICKS - 1)

        held = backward_take(TICKS - 1)
        send_factors()
        spread_last_gradient()
        backward_give(TICKS - 1, held)
        first_products()
        second_products()

        @pl.when(s % 2 == 0)
        def _():
            forward(TICKS - 1)


    factor = 1.0 / (TICKS * replicas)
    at = pl.ds(pl.multiple_of(p * share, 128), share)
    spread_wait(x_refs, 1)
    own = product(0, py)
    swap(0).wait()
    total = own + p_recv[0].astype(F32)
    gw_in_out[...] = (total * (gain_ref[:, at].astype(F32) * factor)).astype(BF16)
    ggain_out[...] = (
        jnp.sum(total * w_in[:, at].astype(F32), axis=0, keepdims=True) * factor
    )
    spread_wait(g_refs, 1)
    own = product(1, py)
    swap(1).wait()
    gw_out_out[...] = ((own + p_recv[1].astype(F32)) * factor).astype(BF16)

    for t in range(TICKS):
        for which, away, _ in direct if t == 0 else ends:

            @pl.when(away)
            def _():
                entry_copy(which, t, 0).wait_send()
                if t > 0:
                    entry_copy(which, t, 1).wait_send()

    for t in range(TICKS - 1):
        for j in range(ring):

            @pl.when(not_last)
            def _():
                y_copy(t, j).wait_send()

            @pl.when(not_first)
            def _():
                d_copy(t, j).wait_send()

    pltpu.make_async_copy(y_send.at[TICKS - 1], fwd_out, out_sem.at[0]).wait()
    pltpu.make_async_copy(d_send.at[TICKS - 1], bwd_out, out_sem.at[1]).wait()


def hand_over(*refs):
    sources, results, held, sem = refs[:5], refs[5:10], refs[10:15], refs[15]
    takes = [
        pltpu.make_async_copy(src, mid, sem.at[0, i])
        for i, (src, mid) in enumerate(zip(sources, held))
    ]
    gives = [
        pltpu.make_async_copy(mid, dst, sem.at[1, i])
        for i, (mid, dst) in enumerate(zip(held, results))
    ]
    for take in takes:
        take.start()
    for take, give in zip(takes, gives):
        take.wait()
        give.start()
    for give in gives:
        give.wait()


def solution(mesh):
    sections = mesh.shape["section"]
    replicas = mesh.shape["dp"]

    def body(
        entry_codes,
        loss_target,
        fwd_inflow,
        bwd_inflow,
        act_cache,
        act_exps,
        grad_cache,
        grad_exps,
        fwd_rows,
        bwd_rows,
        norm_gain,
        w_in,
        w_out,
    ):
        win, width = w_in.shape[1:]
        ring = replicas // 2
        cut = width // ring
        share = width // replicas
        blocks = act_exps.shape[-1]
        full = (ROWS, width)
        dma = pltpu.SemaphoreType.DMA
        hbm = pl.BlockSpec(memory_space=pltpu.HBM)
        vmem = pl.BlockSpec(memory_space=pltpu.VMEM)
        outs = pl.pallas_call(
            functools.partial(kernel, sections, replicas),
            out_shape=(
                jax.ShapeDtypeStruct((win, share), BF16),
                jax.ShapeDtypeStruct((win, share), BF16),
                jax.ShapeDtypeStruct((1, share), F32),
                jax.ShapeDtypeStruct(full, BF16),
                jax.ShapeDtypeStruct(full, BF16),
            ),
            in_specs=[hbm] * 13,
            out_specs=(vmem, vmem, vmem, hbm, hbm),
            scratch_shapes=[
                pltpu.SMEM((1, TICKS), jnp.int32),
                pltpu.SMEM((1, TICKS), jnp.int32),
                pltpu.VMEM((1, width), BF16),
                pltpu.VMEM((TICKS, ROWS, blocks), jnp.int32),
                pltpu.VMEM((TICKS, ROWS, blocks), jnp.int32),
                pltpu.VMEM((2, TICKS) + full, BF16),
                pltpu.VMEM((TICKS,) + full, BF16),
                pltpu.VMEM((win, width), BF16),
                pltpu.VMEM((win, width), BF16),
                pltpu.VMEM((win, width), BF16),
                pltpu.VMEM(full, BF16),
                pltpu.VMEM(full, BF16),
                pltpu.VMEM((TICKS,) + full, BF16),
                pltpu.VMEM((TICKS,) + full, BF16),
                pltpu.VMEM((TICKS,) + full, BF16),
                pltpu.VMEM((TICKS,) + full, BF16),
                pltpu.VMEM(full, BF16),
                pltpu.VMEM((TICKS,) + full, BF16),
                pltpu.VMEM((TICKS,) + full, BF16),
                pltpu.VMEM((TICKS - 1,) + full, BF16),
                pltpu.VMEM((TICKS,) + full, BF16),
                pltpu.VMEM((TICKS - 1,) + full, BF16),
                pltpu.VMEM((TICKS, ROWS, win), F32),
                pltpu.VMEM((TICKS, ROWS, win), F32),
                pltpu.VMEM((TICKS, ROWS, 128), F32),
                pltpu.VMEM((TICKS, ROWS, win), BF16),
                pltpu.VMEM((TICKS, ROWS, win), BF16),
                pltpu.VMEM((2, TICKS, ROWS, win), BF16),
                pltpu.VMEM((ring, TICKS, ROWS, cut), BF16),
                pltpu.VMEM((ring, TICKS, ROWS, cut), BF16),
                pltpu.VMEM((ring, 2, TICKS, ROWS, win), BF16),
                pltpu.VMEM((2, win, share), BF16),
                pltpu.VMEM((2, win, share), BF16),
                dma((11,)),
                pltpu.VMEM((TICKS, ROWS, width // sections), BF16),
                dma((2,)),
                dma((2, TICKS)),
                dma((2, TICKS)),
                dma((TICKS - 1, ring)),
                dma((TICKS - 1, ring)),
                dma((TICKS - 1, ring)),
                dma((TICKS - 1, ring)),
                dma((2 * TICKS, ring)),
                dma((ring, 2 * TICKS)),
                dma((2 * TICKS, ring)),
                dma((ring, 2 * TICKS)),
                dma((ring,)),
                dma((ring,)),
                dma((2,)),
                dma((2,)),
                dma((2,)),
            ],
            compiler_params=pltpu.CompilerParams(
                collective_id=0,
                has_side_effects=True,
                vmem_limit_bytes=VMEM_BYTES,
            ),
        )(
            fwd_rows,
            bwd_rows,
            norm_gain,
            act_exps[0],
            grad_exps[0],
            entry_codes,
            loss_target,
            fwd_inflow[0],
            bwd_inflow[0],
            act_cache[0],
            grad_cache[0],
            w_in[0],
            w_out[0],
        )
        gw_in, gw_out, ggain, fwd_last, bwd_last = pl.pallas_call(
            hand_over,
            out_shape=tuple(jax.ShapeDtypeStruct(o.shape, o.dtype) for o in outs),
            in_specs=[pl.BlockSpec(memory_space=pl.ANY)] * 5,
            out_specs=(hbm,) * 5,
            scratch_shapes=[pltpu.VMEM(o.shape, o.dtype) for o in outs] + [dma((2, 5))],
            compiler_params=pltpu.CompilerParams(vmem_limit_bytes=VMEM_BYTES),
        )(*outs)
        return gw_in[None], gw_out[None], ggain, fwd_last[None], bwd_last[None]

    return jax.shard_map(
        body,
        mesh=mesh,
        in_specs=(
            P(None, "dp", "section"),
            P(None, "dp", "section"),
            P("section", "dp", None),
            P("section", "dp", None),
            P("section", "dp", None, None),
            P("section", "dp", None, None),
            P("section", "dp", None, None),
            P("section", "dp", None, None),
            P("section", "dp"),
            P("section", "dp"),
            P("section", None),
            P("section", None, None),
            P("section", None, None),
        ),
        out_specs=(
            P("section", None, "dp"),
            P("section", None, "dp"),
            P("section", "dp"),
            P("section", "dp", None),
            P("section", "dp", None),
        ),
        check_vma=False,
    )
```

profile of v0, /device:TPU:33, one launch (start us, length us, event | category | flops | bytes accessed | tf_op | source)
XLA Modules:
  0.0 55.5 jit_solution(1754788898342642744)
XLA Ops:
  0.6 52.7 %shard_map.164 = (bf16[64,1536]{1,0:T(8,128)(2,1)}, bf16[64,1536]{1,0:T(8,128)(2,1)}, f32[1,1536]{1,0:T(1,128)}, bf16[16,12288]{1,0:T(8,128)(2,1)}, bf16[16,12288]{1,0:T(8,128)(2,1)}) custom-call(s32[1,4]{1,0:T(1,128)} %fwd_rows_hbm.1, s32[1,4]{1,0:T(1,128)} %bwd_rows_hbm.1, bf16[1,12288]{1,0:T(2,128)(2,1)} %gain_hbm.1, s32[4,16,96]{2,1,0:T(8,128)} %bitcast.18, ...), custom_call_target="tpu_custom_call" | custom-call | tf_op jit(solution)/shard_map/pallas_call | solution.py:852
  53.3 2.2 %shard_map.165 = (bf16[64,1536]{1,0:T(8,128)(2,1)}, bf16[64,1536]{1,0:T(8,128)(2,1)}, f32[1,1536]{1,0:T(1,128)}, bf16[16,12288]{1,0:T(8,128)(2,1)}, bf16[16,12288]{1,0:T(8,128)(2,1)}) custom-call(bf16[64,1536]{1,0:T(8,128)(2,1)} %get-tuple-element.15.refs_0_, bf16[64,1536]{1,0:T(8,128)(2,1)} %get-tuple-element.16.refs_1_, ...), custom_call_target="tpu_custom_call" | custom-call | tf_op jit(solution)/shard_map/pallas_call | solution.py:936
where the time goes:
time: 55.6 us; the launch traced here: 55.5 us
  Pallas kernels  54.8 us (99%)
  between operations  0.65 us (1%)
    pallas_call x1, Pallas kernels, body(): pl.pallas_call(functools.partial(kernel, sections, replicas), out_shape=(...  52.7 us
    pallas_call x1, Pallas kernels, body(): pl.pallas_call(hand_over, out_shape=tuple((jax.ShapeDtypeStruct(o.shape,...  2.18 us

commit v1 on v0

--- a/solution.py
+++ b/solution.py
@@ -366,6 +366,17 @@
     def expand_backward(t):
         expand(grad_exps, bwd_rows, lim_grad, t)
 
+    for i in (6, 7, 9, 10):
+        loads[i].wait()
+
+    @pl.when((s % 2 == 1) | last)
+    def _():
+        expand_forward(0)
+
+    @pl.when((s % 2 == 0) & not_last)
+    def _():
+        expand_backward(0)
+
     loads[1].wait()
     loads[8].wait()
 
@@ -385,8 +396,7 @@
     @pl.when(last)
     def _():
         pass_entries()
-    for i in (0, 6, 7, 9, 10):
-        loads[i].wait()
+    loads[0].wait()
 
     def y_copy(t, j):
         return pltpu.make_async_remote_copy(
@@ -686,7 +696,6 @@
     def _():
         for i in (2, 3, 4, 5):
             loads[i].wait()
-        expand_forward(0)
         forward(0)
         backward(0)
         more_entries(2)
@@ -709,7 +718,6 @@
         def _():
             for i in (2, 3):
                 loads[i].wait()
-            expand_forward(0)
             forward(0)
             pass_entries()
             for i in (4, 5):
@@ -720,10 +728,9 @@
 
         @pl.when(s % 2 == 0)
         def _():
+            prepare_backward()
             for i in (4, 5, 3):
                 loads[i].wait()
-            prepare_backward()
-            expand_backward(0)
             backward(0)
             pass_entries()
             loads[2].wait()

time: 55.6 us -> 55.6 us (level)
  no operation moved by 1% of the time
where the time goes in v1:
time: 55.6 us; the launch traced here: 55.5 us
  Pallas kernels  54.9 us (99%)
  between operations  0.65 us (1%)
    pallas_call x1, Pallas kernels, body(): pl.pallas_call(functools.partial(kernel, sections, replicas), out_shape=(...  52.7 us
    pallas_call x1, Pallas kernels, body(): pl.pallas_call(hand_over, out_shape=tuple((jax.ShapeDtypeStruct(o.shape,...  2.18 us

profile of v1, /device:TPU:33, one launch (start us, length us, event | category | flops | bytes accessed | tf_op | source)
XLA Modules:
  0.0 55.5 jit_solution(457069632800611869)
XLA Ops:
  0.6 52.7 %shard_map.164 = (bf16[64,1536]{1,0:T(8,128)(2,1)}, bf16[64,1536]{1,0:T(8,128)(2,1)}, f32[1,1536]{1,0:T(1,128)}, bf16[16,12288]{1,0:T(8,128)(2,1)}, bf16[16,12288]{1,0:T(8,128)(2,1)}) custom-call(s32[1,4]{1,0:T(1,128)} %fwd_rows_hbm.1, s32[1,4]{1,0:T(1,128)} %bwd_rows_hbm.1, bf16[1,12288]{1,0:T(2,128)(2,1)} %gain_hbm.1, s32[4,16,96]{2,1,0:T(8,128)} %bitcast.18, ...), custom_call_target="tpu_custom_call" | custom-call | tf_op jit(solution)/shard_map/pallas_call | solution.py:859
  53.3 2.2 %shard_map.165 = (bf16[64,1536]{1,0:T(8,128)(2,1)}, bf16[64,1536]{1,0:T(8,128)(2,1)}, f32[1,1536]{1,0:T(1,128)}, bf16[16,12288]{1,0:T(8,128)(2,1)}, bf16[16,12288]{1,0:T(8,128)(2,1)}) custom-call(bf16[64,1536]{1,0:T(8,128)(2,1)} %get-tuple-element.15.refs_0_, bf16[64,1536]{1,0:T(8,128)(2,1)} %get-tuple-element.16.refs_1_, ...), custom_call_target="tpu_custom_call" | custom-call | tf_op jit(solution)/shard_map/pallas_call | solution.py:943
